TPU v7x, 512 devices: a whole 4x4x16 slice. The times are simulated.
512 devices in a mesh: brick: 128 (over z, x, core), slab: 4 (over y).
Axes of the slice: x: 4, y: 4, z: 16, core: 2. Of those that a mesh axis runs over, the one named last changes fastest.
Arguments:
- adjoint_end: float32 [3, 4194304], P(None, ('brick', 'slab')), may hold values from -6 to 6
- positions: float32 [2, 3, 4194304], P(None, None, ('brick', 'slab')), may hold values from 0.5 to 2.5
- tile_brick: int32 [2, 32768], P(None, ('brick', 'slab')), may hold values from 0 to 127
- tile_fill: int32 [32768], P(('brick', 'slab')), may hold values from 4 to 128, as said below
- send_rows: int32 [512, 256], P(('brick', 'slab')), may hold values from 0 to 8192, as said below
- source_rows: int32 [4194304], P(('brick', 'slab')), may hold values from 0 to 8447, as said below
- ckpt_mass: float32 [65536, 128], P(('brick', 'slab')), may hold values from 0.5 to 4
- ckpt_velocity: float32 [65536, 384], P(('brick', 'slab')), may hold values from -6 to 6
- ckpt_target: int32 [65536], P(('brick', 'slab')), may hold values from 0 to 255, as said below
- ckpt_brick: int32 [65536], P(('brick', 'slab')), may hold values from 0 to 127, as said below
- gripper_axis: float32 [3], replicated, may hold values from 0.5 to 1
Outputs:
- adjoint_start: float32 [3, 4194304], P(None, ('brick', 'slab'))
Inputs may be any that keep to these rules, and one draw needn't show every extreme that they name: `tile_fill`: counted from a tile's first row; the first tile of every device is full. `send_rows`: distinct live rows of the device's second layout; the first 128 go to the previous device along brick, the rest to the next; 8192 marks every slot exactly where that neighbour does not exist, and no other. `source_rows`: A row of the first layout takes its own row of the second layout unless that row was sent; each sent row's place takes exactly one received slot, and every received slot from an existing neighbour is used once. Both layouts share tile_fill. `ckpt_target`: values of one device are distinct; the backward owner has the sender's slab index; a device sends 0, 1 or 2 bricks to each peer, in slots from 0. `ckpt_brick`: each backward owner receives each of its 128 bricks exactly once.
All inputs are finite; a program needn't handle non-finite values.
Results may differ from a plain program's by a relative error of at most 0.00065.
Values sent between devices are 32-bit elements; how exact they have to be, the bound alone decides.
A program may use at most 64 MiB of HBM per device.

v0:
```python
import jax
import jax.numpy as jnp
from jax import lax
from jax.experimental import pallas as pl
from jax.experimental.pallas import tpu as pltpu
from jax.sharding import PartitionSpec as P

TILE = 128
TILES = 64
GROUPS = 8
NZ = 16
NXC = 8
N_BRICK = 128
N_SLAB = 4
BLOCK = 40

diffusion = 0.15
F32 = jnp.float32
BF16 = jnp.bfloat16
MESH = pl.DeviceIdType.MESH


def contract_last(left, right):
    return lax.dot_general(left, right, (((1,), (1,)), ((), ())), preferred_element_type=F32)


def contract_first(left, right):
    return lax.dot_general(left, right, (((0,), (0,)), ((), ())), preferred_element_type=F32)


def split(value):
    high = value.astype(BF16)
    low = (value - high.astype(F32)).astype(BF16)
    return high, low


def iota(shape, dim):
    return lax.broadcasted_iota(jnp.int32, shape, dim)


def bspline(offset):
    magnitude = jnp.abs(offset)
    inner = 0.75 - offset * offset
    tail = 1.5 - magnitude
    outer = 0.5 * tail * tail
    return jnp.where(magnitude < 0.5, inner, jnp.where(magnitude < 1.5, outer, 0.0))


def kernel(
    adj_ref, pos_ref, tile_ref, fill_ref, send_ref, source_ref, mass_ref, vel_ref,
    target_ref, brick_ref, axis_ref, out_ref,
    weights, rows, per_tile, grid, xsum, ext,
    s1a, r1a, s1b, r1b, s2a, r2a, s2b, r2b,
    xs, xr, ys, yr, ms, mr,
    a1s, a1r, b1s, b1r, a2s, a2r, b2s, b2r, hs, hr, gs, gr,
):
    b = lax.axis_index("brick")
    s = lax.axis_index("slab")
    z = lax.div(b, NXC)
    xc = lax.rem(b, NXC)
    left = lax.rem(b + N_BRICK - 1, N_BRICK)
    right = lax.rem(b + 1, N_BRICK)
    down = lax.rem(s + N_SLAB - 1, N_SLAB)
    up = lax.rem(s + 1, N_SLAB)

    def near(d):
        return lax.rem(xc + d, NXC)

    def far(d):
        return lax.rem(z + d, NZ)

    barrier = pltpu.get_barrier_semaphore()

    def greet_near(d, carry):
        pl.semaphore_signal(barrier, inc=1, device_id=(z * NXC + near(d), s), device_id_type=MESH)
        return carry

    def greet_far(d, carry):
        pl.semaphore_signal(barrier, inc=1, device_id=(far(d) * NXC + xc, s), device_id_type=MESH)
        return carry

    lax.fori_loop(1, NXC, greet_near, 0)
    lax.fori_loop(1, NZ, greet_far, 0)
    for who in ((left, s), (right, s), (b, down), (b, up)):
        pl.semaphore_signal(barrier, inc=1, device_id=who, device_id_type=MESH)

    def remote(src, dst, send, recv, who):
        return pltpu.make_async_remote_copy(
            src_ref=src, dst_ref=dst, send_sem=send, recv_sem=recv, device_id=who,
            device_id_type=MESH,
        )

    def near_copy(src, dst, send, recv, d):
        to = near(d)
        return remote(
            src.at[pl.ds(pl.multiple_of(to * BLOCK, 8), BLOCK)],
            dst.at[pl.ds(pl.multiple_of(xc * BLOCK, 8), BLOCK)],
            send.at[d], recv.at[d], (z * NXC + to, s),
        )

    def far_copy(src, dst, send, recv, d):
        to = far(d)
        return remote(src.at[to], dst.at[z], send.at[d], recv.at[d], (to * NXC + xc, s))

    def run(count, act):
        def body(d, carry):
            act(d)
            return carry

        lax.fori_loop(1, count, body, 0)

    lane = iota((8, 128), 1)
    axis = [jnp.full((1, 128), axis_ref[c], F32) for c in range(3)]
    length = jnp.sqrt(axis[0] * axis[0] + axis[1] * axis[1] + axis[2] * axis[2])
    normal = [a / length for a in axis]
    lane_q = iota((128, 128), 1)
    v0 = vel_ref[:, 0:128]
    v1 = vel_ref[:, 128:256]
    v2 = vel_ref[:, 256:384]
    speed_first = normal[0] * v0 + normal[1] * pltpu.roll(v0, 64, 1) + normal[2] * v1
    speed_second = normal[0] * v1 + normal[1] * pltpu.roll(v2, 64, 1) + normal[2] * v2
    speed = jnp.where(lane_q < 64, speed_first, speed_second)
    contact = jnp.where(speed < 0.0, 1.0, 0.0)
    mass_turned = pltpu.roll(mass_ref[...], 64, 1)
    packed_a = jnp.where(lane_q < 64, mass_turned, contact)
    packed_b = jnp.where(lane_q < 64, contact, mass_turned)
    both = jnp.concatenate([packed_a, packed_b], axis=1)
    high, low = split(both)
    target = target_ref[...]
    slot = lax.bitwise_and(target, 1)
    peer = lax.shift_right_logical(target, 1)
    peer_near = lax.bitwise_and(peer, NXC - 1)
    within = slot * NZ + lax.shift_right_logical(peer, 3)
    place = peer_near * 32 + within
    chosen = jnp.where(iota((256, 128), 0) == place, 1.0, 0.0).astype(BF16)
    packed = jnp.dot(
        jnp.concatenate([chosen, chosen], axis=1), jnp.concatenate([high, low], axis=0),
        preferred_element_type=F32,
    )
    index_left = jnp.where(
        iota((16, 128), 0) == peer_near, (brick_ref[...] + 1).astype(F32), 0.0
    ).astype(BF16)
    index_right = jnp.where(iota((128, 128), 0) == within, 1.0, 0.0).astype(BF16)
    index_out = contract_last(index_left, index_right)
    for i in range(NXC):
        s1a[BLOCK * i:BLOCK * i + 32, :] = packed[32 * i:32 * i + 32, 0:128]
        s1a[BLOCK * i + 32:BLOCK * i + 40, :] = jnp.broadcast_to(index_out[i:i + 1], (8, 128))
        s1b[BLOCK * i:BLOCK * i + 32, :] = packed[32 * i:32 * i + 32, 128:256]
        s1b[BLOCK * i + 32:BLOCK * i + 40, :] = jnp.zeros((8, 128), F32)

    pl.semaphore_wait(barrier, NXC - 1 + NZ - 1 + 4)
    run(NXC, lambda d: near_copy(s1a, r1a, a1s, a1r, d).start())
    run(NXC, lambda d: near_copy(s1b, r1b, b1s, b1r, d).start())
    own = pl.ds(pl.multiple_of(xc * BLOCK, 8), BLOCK)
    r1a[own] = s1a[own]
    r1b[own] = s1b[own]

    def spread(t, carry):
        block = adj_ref[:, pl.ds(pl.multiple_of(t * TILE, TILE), TILE)]
        for c in range(3):
            rows[c, pl.ds(t, 1), :] = block[c:c + 1]
        return carry

    lax.fori_loop(0, TILES, spread, 0, unroll=8)

    sub = iota((8, 128), 0)
    node_x = lax.bitwise_and(sub, 3).astype(F32)
    node_y = lax.shift_right_logical(sub, 2).astype(F32)
    row48 = lax.bitwise_and(iota((48, 128), 0), 7)

    def build(k, g):
        for i in range(8):
            t = g * 8 + i
            at = pl.ds(pl.multiple_of(t * TILE, TILE), TILE)
            pz, py, px = (
                jnp.broadcast_to(pos_ref[k, c:c + 1, at], (8, 128)) for c in range(3)
            )
            pz = jnp.where(lane < fill_ref[0, t], pz, 100.0)
            wx = bspline(px - node_x)
            wz = bspline(pz - node_x)
            xy = [bspline(py - node_y) * wx, bspline(py - (node_y + 2.0)) * wx]
            value = jnp.concatenate(
                [jnp.broadcast_to(wz[n:n + 1], (8, 128)) * xy[h] for n in range(4) for h in range(2)],
                axis=0,
            )
            high, low = split(value)
            weights[k, t, :, 0:128] = high
            weights[k, t, :, 128:256] = low

    def to_grid(k, g):
        at = pl.ds(pl.multiple_of(g * 8, 8), 8)
        parts = [rows[c, at, :] for c in range(3)]
        value = jnp.concatenate(parts, axis=0)
        high = value.astype(BF16).astype(F32)
        value = jnp.concatenate([high, value - high], axis=0)
        lhs = jnp.concatenate(
            [jnp.where(row48 == i, value, 0.0).astype(BF16) for i in range(8)], axis=1
        )
        rhs = jnp.concatenate(
            [
                jnp.concatenate(
                    [weights[k, g * 8 + i, :, 0:128], weights[k, g * 8 + i, :, 128:256]], axis=0
                )
                for i in range(8)
            ],
            axis=1,
        )
        found = contract_last(lhs, rhs)
        found = found[0:24] + found[24:48]
        for c in range(3):
            per_tile[c, at, :] = found[8 * c:8 * c + 8]

    def table(k):
        line = jnp.broadcast_to(tile_ref[k:k + 1, :].astype(F32), (TILES, TILES))
        mine = iota((TILES, TILES), 0) == iota((TILES, TILES), 1)
        column = jnp.sum(jnp.where(mine, line, 0.0), axis=1, keepdims=True)
        return jnp.where(iota((TILES, 128), 1).astype(F32) == column, 1.0, 0.0).astype(BF16)

    def sum_bricks(tiles):
        value = jnp.concatenate([per_tile[c] for c in range(3)], axis=1)
        high, low = split(value)
        found = contract_first(
            jnp.concatenate([high, low], axis=0), jnp.concatenate([tiles, tiles], axis=0)
        )
        for c in range(3):
            grid[64 * c:64 * c + 64, :] = (
                found[128 * c:128 * c + 64] + found[128 * c + 64:128 * c + 128]
            )

    def halo(k):
        x_high = remote(xs.at[k, 0], xr.at[k, 0], hs.at[k, 0], hr.at[k, 0], (right, s))
        x_low = remote(xs.at[k, 1], xr.at[k, 1], hs.at[k, 1], hr.at[k, 1], (left, s))
        y_high = remote(ys.at[k, 0], yr.at[k, 0], hs.at[k, 2], hr.at[k, 2], (b, up))
        y_low = remote(ys.at[k, 1], yr.at[k, 1], hs.at[k, 3], hr.at[k, 3], (b, down))
        return x_high, x_low, y_high, y_low

    def send_halo(k):
        xs[k, 0] = grid[pl.ds(3, 48, stride=4), :]
        xs[k, 1] = grid[pl.ds(0, 48, stride=4), :]
        cells = grid[...].reshape(12, 16, 128)
        ys[k, 0] = cells[:, 12:16]
        ys[k, 1] = cells[:, 0:4]
        for copy in halo(k):
            copy.start()

    brick_lane = iota((1, 128), 1)
    lane_x = lax.bitwise_and(brick_lane, 7)
    lane_y = lax.bitwise_and(lax.shift_right_logical(brick_lane, 3), 3)
    lane_z = lax.shift_right_logical(brick_lane, 5)
    has_left = jnp.where(b > 0, 1.0, 0.0)
    has_right = jnp.where(b < N_BRICK - 1, 1.0, 0.0)
    has_down = jnp.where(s > 0, 1.0, 0.0)
    has_up = jnp.where(s < N_SLAB - 1, 1.0, 0.0)

    def smooth(k):
        planes = [grid[pl.ds(j, 48, stride=4), :] for j in range(4)]
        before = jnp.where(
            lane_x == 0, pltpu.roll(xr[k, 0] * has_left, 121, 1), pltpu.roll(planes[3], 1, 1)
        )
        after = jnp.where(
            lane_x == 7, pltpu.roll(xr[k, 1] * has_right, 7, 1), pltpu.roll(planes[0], 127, 1)
        )
        line = [before] + planes + [after]
        for j in range(4):
            xsum[pl.ds(j, 48, stride=4), :] = line[j] + line[j + 2]
        cells = grid[...].reshape(12, 16, 128)
        low = pltpu.roll((yr[k, 0] * has_down), 104, 2)
        high = pltpu.roll((yr[k, 1] * has_up), 24, 2)
        lane_y3 = lane_y.reshape(1, 1, 128)
        below = jnp.where(lane_y3 == 0, low, pltpu.roll(cells[:, 12:16], 8, 2))
        above = jnp.where(lane_y3 == 3, high, pltpu.roll(cells[:, 0:4], 120, 2))
        ysum = jnp.concatenate([cells[:, 4:16], above], axis=1) + jnp.concatenate(
            [below, cells[:, 0:12]], axis=1
        )
        out = []
        for c in range(3):
            base = grid[64 * c:64 * c + 64, :]
            last = jnp.where(lane_z == 0, 0.0, pltpu.roll(base[48:64], 32, 1))
            first = jnp.where(lane_z == 3, 0.0, pltpu.roll(base[0:16], 96, 1))
            zsum = jnp.concatenate([base[16:64], first], axis=0) + jnp.concatenate(
                [last, base[0:48]], axis=0
            )
            beside = (
                xsum[64 * c:64 * c + 64, :] + ysum[4 * c:4 * c + 4].reshape(64, 128) + zsum
            )
            out.append(base + diffusion * (beside - 6.0 * base))
        return out

    def relay(src, dst):
        for i in range(NZ):
            dst[i, 0:8, :] = src[pl.ds(i, 8, stride=BLOCK), :]
            dst[i, 8:16, :] = src[pl.ds(16 + i, 8, stride=BLOCK), :]

    def by_node(got, place):
        value = got.reshape(256, 128)
        high, low = split(value)
        return contract_first(
            jnp.concatenate([high, low], axis=0), jnp.concatenate([place, place], axis=0)
        )

    def correct(cells, mass, touch, tiles):
        project = normal[0] * cells[0] + normal[1] * cells[1] + normal[2] * cells[2]
        scaled = [(cells[c] - touch * normal[c] * project) / mass for c in range(3)]
        highs, lows = zip(*(split(value) for value in scaled))
        stack = jnp.concatenate(
            [part for half in (highs, lows) for value in half for part in (value, value)], axis=0
        )
        found = contract_last(tiles, stack)
        for i in range(6):
            ext[i] = found[:, 128 * i:128 * i + 128]

    pair_of = lax.bitwise_and(iota((8, 128), 0), 7) * 64
    lane_pair = lax.bitwise_and(lane, 64)

    def to_rows(k, g):
        at = pl.ds(pl.multiple_of(g * 8, 8), 8)
        parts = [ext[i, at, :] for i in range(6)]
        lhs = jnp.concatenate(
            [
                jnp.concatenate(
                    [jnp.where(pair_of == lane_pair + 128 * j, part, 0.0) for part in parts], axis=0
                ).astype(BF16)
                for j in range(4)
            ],
            axis=1,
        )
        rhs = jnp.concatenate([weights[k, g * 8 + i] for i in range(8)], axis=0)
        found = jnp.dot(lhs, rhs, preferred_element_type=F32)
        return found[0:24, 0:128] + found[24:48, 0:128] + found[0:24, 128:256]

    def first_pass(g, carry):
        build(1, g)
        to_grid(1, g)
        return carry

    lax.fori_loop(0, GROUPS, first_pass, 0)
    tiles_b = table(1)
    sum_bricks(tiles_b)
    send_halo(1)

    run(NXC, lambda d: near_copy(s1a, r1a, a1s, a1r, d).wait_recv())
    relay(r1a, s2a)
    index_in = r1a[pl.ds(32, 8, stride=BLOCK), :]
    index_two = jnp.concatenate([index_in, pltpu.roll(index_in, 112, 1)], axis=0)
    index_two = jnp.where(iota((16, 128), 1) < NZ, index_two, 0.0).astype(BF16)
    pick = jnp.where(iota((NZ, 128), 0) == iota((NZ, 128), 1), 1.0, 0.0).astype(BF16)
    index_far = contract_last(
        pick, jnp.concatenate([index_two, jnp.zeros((112, 128), BF16)], axis=0)
    )
    for i in range(NZ):
        s2a[i, 16:17, :] = index_far[i:i + 1]
    run(NZ, lambda d: far_copy(s2a, r2a, a2s, a2r, d).start())
    r2a[z] = s2a[z]

    def second_weights(g, carry):
        build(0, g)
        return carry

    lax.fori_loop(0, GROUPS, second_weights, 0)
    tiles_a = table(0)

    for copy in halo(1):
        copy.wait_recv()
    cells = smooth(1)

    run(NXC, lambda d: near_copy(s1b, r1b, b1s, b1r, d).wait_recv())
    relay(r1b, s2b)
    r2b[z] = s2b[z]

    run(NZ, lambda d: far_copy(s2a, r2a, a2s, a2r, d).wait_recv())
    run(NZ, lambda d: far_copy(s2b, r2b, b2s, b2r, d).start())
    index_row = jnp.concatenate([r2a[i, 16:17, :] for i in range(NZ)], axis=0)
    spread_index = jnp.concatenate(
        [jnp.broadcast_to(index_row[i:i + 1], (16, 128)) for i in range(NZ)], axis=0
    )
    mine = lax.bitwise_and(iota((256, 128), 0), 15) == iota((256, 128), 1)
    column = jnp.sum(jnp.where(mine, spread_index, 0.0), axis=1, keepdims=True) - 1.0
    placed = jnp.where(iota((256, 128), 1).astype(F32) == column, 1.0, 0.0).astype(BF16)
    nodes_b = by_node(jnp.concatenate([r2a[i, 0:16, :] for i in range(NZ)], axis=0), placed)
    correct(cells, nodes_b[0:64], nodes_b[64:128], tiles_b)

    def second_rows(g, carry):
        found = to_rows(1, g)
        for c in range(3):
            rows[c, pl.ds(pl.multiple_of(g * 8, 8), 8), :] = found[8 * c:8 * c + 8]
        return carry

    lax.fori_loop(0, GROUPS, second_rows, 0)

    for side in range(2):
        wanted = send_ref[:, 128 * side:128 * side + 128]
        which = jnp.broadcast_to(lax.bitwise_and(wanted, 127), (8, 128))
        tile = lax.shift_right_logical(wanted, 7)
        for c in range(3):
            total = jnp.zeros((8, 128), F32)
            for v in range(8):
                found = jnp.take_along_axis(
                    rows[c, 8 * v:8 * v + 8, :], which, axis=1, mode="promise_in_bounds"
                )
                total = total + jnp.where(sub + 8 * v == tile, found, 0.0)
            ms[side, c:c + 1, :] = jnp.sum(total, axis=0, keepdims=True)
    go_left = remote(ms.at[0], mr.at[1], gs.at[0], gr.at[0], (left, s))
    go_right = remote(ms.at[1], mr.at[0], gs.at[1], gr.at[1], (right, s))
    go_left.start()
    go_right.start()
    go_left.wait_recv()
    go_right.wait_recv()
    for v in range(8):
        source = source_ref[8 * v:8 * v + 8, :]
        which = lax.bitwise_and(source, 127)
        for c in range(3):
            at_left, at_right = (
                jnp.take_along_axis(
                    jnp.broadcast_to(mr[side, c:c + 1, :], (8, 128)), which, axis=1,
                    mode="promise_in_bounds",
                )
                for side in range(2)
            )
            kept = rows[c, 8 * v:8 * v + 8, :]
            rows[c, 8 * v:8 * v + 8, :] = jnp.where(
                source < 8192, kept, jnp.where(source < 8320, at_left, at_right)
            )

    def third_pass(g, carry):
        to_grid(0, g)
        return carry

    lax.fori_loop(0, GROUPS, third_pass, 0)
    sum_bricks(tiles_a)
    send_halo(0)
    run(NZ, lambda d: far_copy(s2b, r2b, b2s, b2r, d).wait_recv())
    nodes_a = by_node(r2b[...], placed)
    for copy in halo(0):
        copy.wait_recv()
    correct(smooth(0), nodes_a[64:128], nodes_a[0:64], tiles_a)

    def last_rows(g, carry):
        found = to_rows(0, g)
        for i in range(8):
            at = pl.ds(pl.multiple_of((g * 8 + i) * TILE, TILE), TILE)
            for c in range(3):
                out_ref[c:c + 1, at] = found[8 * c + i:8 * c + i + 1]
        return carry

    lax.fori_loop(0, GROUPS, last_rows, 0)

    run(NXC, lambda d: near_copy(s1a, r1a, a1s, a1r, d).wait_send())
    run(NXC, lambda d: near_copy(s1b, r1b, b1s, b1r, d).wait_send())
    run(NZ, lambda d: far_copy(s2a, r2a, a2s, a2r, d).wait_send())
    run(NZ, lambda d: far_copy(s2b, r2b, b2s, b2r, d).wait_send())
    for copy in halo(1) + halo(0) + (go_left, go_right):
        copy.wait_send()


def per_device(
    adjoint_end, positions, tile_brick, tile_fill, send_rows, source_rows,
    ckpt_mass, ckpt_velocity, ckpt_target, ckpt_brick, gripper_axis,
):
    vmem = pl.BlockSpec(memory_space=pltpu.VMEM)
    smem = pl.BlockSpec(memory_space=pltpu.SMEM)
    dma = pltpu.SemaphoreType.DMA
    return pl.pallas_call(
        kernel,
        out_shape=jax.ShapeDtypeStruct((3, TILES * TILE), F32),
        in_specs=[vmem, vmem, vmem, smem, vmem, vmem, vmem, vmem, vmem, vmem, smem],
        out_specs=vmem,
        scratch_shapes=[
            pltpu.VMEM((2, TILES, 64, 256), BF16),
            pltpu.VMEM((3, TILES, TILE), F32),
            pltpu.VMEM((3, TILES, 128), F32),
            pltpu.VMEM((192, 128), F32),
            pltpu.VMEM((192, 128), F32),
            pltpu.VMEM((6, TILES, 128), F32),
            pltpu.VMEM((NXC * BLOCK, 128), F32),
            pltpu.VMEM((NXC * BLOCK, 128), F32),
            pltpu.VMEM((NXC * BLOCK, 128), F32),
            pltpu.VMEM((NXC * BLOCK, 128), F32),
            pltpu.VMEM((NZ, 17, 128), F32),
            pltpu.VMEM((NZ, 17, 128), F32),
            pltpu.VMEM((NZ, 16, 128), F32),
            pltpu.VMEM((NZ, 16, 128), F32),
            pltpu.VMEM((2, 2, 48, 128), F32),
            pltpu.VMEM((2, 2, 48, 128), F32),
            pltpu.VMEM((2, 2, 12, 4, 128), F32),
            pltpu.VMEM((2, 2, 12, 4, 128), F32),
            pltpu.VMEM((2, 3, 128), F32),
            pltpu.VMEM((2, 3, 128), F32),
            dma((NXC,)), dma((NXC,)), dma((NXC,)), dma((NXC,)),
            dma((NZ,)), dma((NZ,)), dma((NZ,)), dma((NZ,)),
            dma((2, 4)), dma((2, 4)), dma((2,)), dma((2,)),
        ],
        compiler_params=pltpu.CompilerParams(
            collective_id=0, has_side_effects=True, vmem_limit_bytes=48 * 1024 * 1024
        ),
        cost_estimate=pl.CostEstimate(
            flops=200_000_000, bytes_accessed=1_000_000, transcendentals=0
        ),
        name="substeps",
    )(
        adjoint_end, positions, tile_brick, tile_fill.reshape(1, TILES), send_rows,
        source_rows.reshape(TILES, TILE), ckpt_mass, ckpt_velocity,
        ckpt_target.reshape(1, 128), ckpt_brick.reshape(1, 128), gripper_axis,
    )


def solution(mesh):
    return jax.shard_map(
        per_device,
        mesh=mesh,
        in_specs=(
            P(None, ("brick", "slab")),
            P(None, None, ("brick", "slab")),
            P(None, ("brick", "slab")),
            P(("brick", "slab")),
            P(("brick", "slab"), None),
            P(("brick", "slab")),
            P(("brick", "slab"), None),
            P(("brick", "slab"), None),
            P(("brick", "slab")),
            P(("brick", "slab")),
            P(),
        ),
        out_specs=P(None, ("brick", "slab")),
        check_vma=False,
    )
```

profile of v0, /device:TPU:24, one launch (start us, length us, event | category | flops | bytes accessed | tf_op | source)
XLA Modules:
  0.0 47.8 jit_solution(6251068821005907330)
XLA Ops:
  0.0 0.0 copy-start
  0.0 0.0 copy-start.1
  0.0 0.0 copy-start.2
  0.0 0.0 copy-start.3
  0.0 0.0 copy-start.4
  0.0 0.0 copy-start.5
  0.0 0.0 copy-start.6
  0.0 0.0 copy-start.7
  0.1 0.0 copy-start.8
  0.1 0.0 copy-start.9
  0.1 1.2 %copy.12.pos_ref = f32[2,3,8192]{2,1,0:T(4,128)S(1)} copy(f32[2,3,8192]{2,0,1:T(2,128)} %param.12) | data formatting | bytes 393216 | tf_op args[1]
  1.3 0.0 copy-done
  1.3 0.0 copy-done.1
  1.3 0.0 copy-done.2
  1.3 0.0 copy-done.3
  1.3 0.0 copy-done.4
  1.3 0.0 copy-done.5
  1.3 0.0 copy-done.6
  1.3 0.0 copy-done.7
  1.3 0.0 copy-done.8
  1.3 0.0 copy-done.9
  1.4 45.8 %substeps.1 = f32[3,8192]{1,0:T(4,128)S(1)} custom-call(f32[3,8192]{1,0:T(4,128)S(1)} %copy-done.1, f32[2,3,8192]{2,1,0:T(4,128)S(1)} %copy.12.pos_ref, s32[2,64]{1,0:T(2,128)S(1)} %copy-done.4, s32[1,64]{1,0:T(1,128)S(1)} %bitcast.5, s32[1,256]{1,0:T(1,128)S(1)} %copy-done.5, s32[64,128]{1,0:T(8,128)S(1)} %bitcast.4, f32[128,128]{1,0:T(8,128)S(1)} %copy-done.2, ...), custom_call_target="tpu_custom_call" | custom-call | flops 200000000 | bytes 1000000 | tf_op jit(solution)/shard_map/substeps/pallas_call | solution.py:462
  47.2 0.7 %copy.14 = f32[3,8192]{1,0:T(4,128)} copy(f32[3,8192]{1,0:T(4,128)S(1)} %substeps.1) | data formatting | bytes 196608
Async XLA Ops:
  0.0 1.3 %copy-start = (f32[128,384]{1,0:T(8,128)S(1)}, f32[128,384]{1,0:T(8,128)}, u32[]{:S(2)}) copy-start(f32[128,384]{1,0:T(8,128)} %vel_ref.1) | copy-start | bytes 589828
  0.0 1.3 %copy-start.1 = (f32[3,8192]{1,0:T(4,128)S(1)}, f32[3,8192]{1,0:T(4,128)}, u32[]{:S(2)}) copy-start(f32[3,8192]{1,0:T(4,128)} %adj_ref.1) | copy-start | bytes 294916
  0.0 1.3 %copy-start.2 = (f32[128,128]{1,0:T(8,128)S(1)}, f32[128,128]{1,0:T(8,128)}, u32[]{:S(2)}) copy-start(f32[128,128]{1,0:T(8,128)} %mass_ref.1) | copy-start | bytes 196612
  0.0 1.3 %copy-start.3 = (s32[8192]{0:T(1024)S(1)}, s32[8192]{0:T(1024)}, u32[]{:S(2)}) copy-start(s32[8192]{0:T(1024)} %param.16) | copy-start | bytes 98308
  0.0 1.3 %copy-start.4 = (s32[2,64]{1,0:T(2,128)S(1)}, s32[2,64]{1,0:T(2,128)}, u32[]{:S(2)}) copy-start(s32[2,64]{1,0:T(2,128)} %tile_ref.1) | copy-start | bytes 1540
  0.0 1.3 %copy-start.5 = (s32[1,256]{1,0:T(1,128)S(1)}, s32[1,256]{1,0:T(1,128)}, u32[]{:S(2)}) copy-start(s32[1,256]{1,0:T(1,128)} %send_ref.1) | copy-start | bytes 3076
  0.0 1.3 %copy-start.6 = (s32[64]{0:T(128)S(1)}, s32[64]{0:T(128)}, u32[]{:S(2)}) copy-start(s32[64]{0:T(128)} %param.14) | copy-start | bytes 772
  0.0 1.3 %copy-start.7 = (s32[128]{0:T(128)S(1)}, s32[128]{0:T(128)}, u32[]{:S(2)}) copy-start(s32[128]{0:T(128)} %param.19) | copy-start | bytes 1540
  0.1 1.3 %copy-start.8 = (s32[128]{0:T(128)S(1)}, s32[128]{0:T(128)}, u32[]{:S(2)}) copy-start(s32[128]{0:T(128)} %param.20) | copy-start | bytes 1540
  0.1 1.3 %copy-start.9 = (f32[3]{0:T(128)S(1)}, f32[3]{0:T(128)}, u32[]{:S(2)}) copy-start(f32[3]{0:T(128)} %axis_ref.1) | copy-start | bytes 40
where the time goes:
time: 47.9 us; the launch traced here: 47.8 us
  Pallas kernels  45.8 us (96%)
  local copies, waits for them, and re-layouts  1.87 us (4%)
    pallas_call x1, Pallas kernels, per_device(): pl.pallas_call(kernel, out_shape=jax.ShapeDtypeStruct((3, TILES * TILE),...  45.8 us
    unnamed x22, local copies, waits for them, and re-layouts  1.87 us

commit v1 on v0

--- a/solution.py
+++ b/solution.py
@@ -47,8 +47,10 @@
 
 
 def kernel(
+    adj_hbm, pos_hbm, tile_hbm, fill_hbm, send_hbm, source_hbm, mass_hbm, vel_hbm,
+    target_hbm, brick_hbm, axis_hbm, out_ref,
     adj_ref, pos_ref, tile_ref, fill_ref, send_ref, source_ref, mass_ref, vel_ref,
-    target_ref, brick_ref, axis_ref, out_ref,
+    target_ref, brick_ref, axis_ref, load_sem,
     weights, rows, per_tile, grid, xsum, ext,
     s1a, r1a, s1b, r1b, s2a, r2a, s2b, r2b,
     xs, xr, ys, yr, ms, mr,
@@ -67,7 +69,8 @@
         return lax.rem(xc + d, NXC)
 
     def far(d):
-        return lax.rem(z + d, NZ)
+        turn = lax.div(d, 2) * (1 - 2 * lax.rem(d, 2))
+        return lax.rem(z + NZ + NZ // 2 + turn, NZ)
 
     barrier = pltpu.get_barrier_semaphore()
 
@@ -79,10 +82,24 @@
         pl.semaphore_signal(barrier, inc=1, device_id=(far(d) * NXC + xc, s), device_id_type=MESH)
         return carry
 
+    lax.fori_loop(1, NZ, greet_far, 0)
     lax.fori_loop(1, NXC, greet_near, 0)
-    lax.fori_loop(1, NZ, greet_far, 0)
     for who in ((left, s), (right, s), (b, down), (b, up)):
         pl.semaphore_signal(barrier, inc=1, device_id=who, device_id_type=MESH)
+
+    loads = [
+        pltpu.make_async_copy(src, dst, load_sem.at[i])
+        for i, (src, dst) in enumerate((
+            (axis_hbm, axis_ref), (vel_hbm, vel_ref), (mass_hbm, mass_ref),
+            (target_hbm, target_ref), (brick_hbm, brick_ref), (adj_hbm, adj_ref),
+            (pos_hbm, pos_ref), (fill_hbm, fill_ref), (tile_hbm, tile_ref),
+            (send_hbm, send_ref), (source_hbm, source_ref),
+        ))
+    ]
+    for load in loads:
+        load.start()
+    for load in loads[0:5]:
+        load.wait()
 
     def remote(src, dst, send, recv, who):
         return pltpu.make_async_remote_copy(
@@ -110,7 +127,7 @@
         lax.fori_loop(1, count, body, 0)
 
     lane = iota((8, 128), 1)
-    axis = [jnp.full((1, 128), axis_ref[c], F32) for c in range(3)]
+    axis = [jnp.full((1, 128), axis_ref[0, c], F32) for c in range(3)]
     length = jnp.sqrt(axis[0] * axis[0] + axis[1] * axis[1] + axis[2] * axis[2])
     normal = [a / length for a in axis]
     lane_q = iota((128, 128), 1)
@@ -155,6 +172,9 @@
     r1a[own] = s1a[own]
     r1b[own] = s1b[own]
 
+    for load in loads[5:11]:
+        load.wait()
+
     def spread(t, carry):
         block = adj_ref[:, pl.ds(pl.multiple_of(t * TILE, TILE), TILE)]
         for c in range(3):
@@ -173,7 +193,7 @@
             t = g * 8 + i
             at = pl.ds(pl.multiple_of(t * TILE, TILE), TILE)
             pz, py, px = (
-                jnp.broadcast_to(pos_ref[k, c:c + 1, at], (8, 128)) for c in range(3)
+                jnp.broadcast_to(pos_ref[c, k:k + 1, at], (8, 128)) for c in range(3)
             )
             pz = jnp.where(lane < fill_ref[0, t], pz, 100.0)
             wx = bspline(px - node_x)
@@ -333,7 +353,7 @@
         to_grid(1, g)
         return carry
 
-    lax.fori_loop(0, GROUPS, first_pass, 0)
+    lax.fori_loop(0, GROUPS, first_pass, 0, unroll=2)
     tiles_b = table(1)
     sum_bricks(tiles_b)
     send_halo(1)
@@ -352,23 +372,24 @@
     run(NZ, lambda d: far_copy(s2a, r2a, a2s, a2r, d).start())
     r2a[z] = s2a[z]
 
+    run(NXC, lambda d: near_copy(s1b, r1b, b1s, b1r, d).wait_recv())
+    relay(r1b, s2b)
+    r2b[z] = s2b[z]
+    run(NZ, lambda d: far_copy(s2b, r2b, b2s, b2r, d).start())
+
     def second_weights(g, carry):
         build(0, g)
         return carry
 
-    lax.fori_loop(0, GROUPS, second_weights, 0)
+    lax.fori_loop(0, GROUPS, second_weights, 0, unroll=2)
     tiles_a = table(0)
 
     for copy in halo(1):
         copy.wait_recv()
     cells = smooth(1)
 
-    run(NXC, lambda d: near_copy(s1b, r1b, b1s, b1r, d).wait_recv())
-    relay(r1b, s2b)
-    r2b[z] = s2b[z]
 
     run(NZ, lambda d: far_copy(s2a, r2a, a2s, a2r, d).wait_recv())
-    run(NZ, lambda d: far_copy(s2b, r2b, b2s, b2r, d).start())
     index_row = jnp.concatenate([r2a[i, 16:17, :] for i in range(NZ)], axis=0)
     spread_index = jnp.concatenate(
         [jnp.broadcast_to(index_row[i:i + 1], (16, 128)) for i in range(NZ)], axis=0
@@ -385,7 +406,7 @@
             rows[c, pl.ds(pl.multiple_of(g * 8, 8), 8), :] = found[8 * c:8 * c + 8]
         return carry
 
-    lax.fori_loop(0, GROUPS, second_rows, 0)
+    lax.fori_loop(0, GROUPS, second_rows, 0, unroll=8)
 
     for side in range(2):
         wanted = send_ref[:, 128 * side:128 * side + 128]
@@ -425,7 +446,7 @@
         to_grid(0, g)
         return carry
 
-    lax.fori_loop(0, GROUPS, third_pass, 0)
+    lax.fori_loop(0, GROUPS, third_pass, 0, unroll=8)
     sum_bricks(tiles_a)
     send_halo(0)
     run(NZ, lambda d: far_copy(s2b, r2b, b2s, b2r, d).wait_recv())
@@ -442,7 +463,7 @@
                 out_ref[c:c + 1, at] = found[8 * c + i:8 * c + i + 1]
         return carry
 
-    lax.fori_loop(0, GROUPS, last_rows, 0)
+    lax.fori_loop(0, GROUPS, last_rows, 0, unroll=8)
 
     run(NXC, lambda d: near_copy(s1a, r1a, a1s, a1r, d).wait_send())
     run(NXC, lambda d: near_copy(s1b, r1b, b1s, b1r, d).wait_send())
@@ -456,15 +477,26 @@
     adjoint_end, positions, tile_brick, tile_fill, send_rows, source_rows,
     ckpt_mass, ckpt_velocity, ckpt_target, ckpt_brick, gripper_axis,
 ):
-    vmem = pl.BlockSpec(memory_space=pltpu.VMEM)
-    smem = pl.BlockSpec(memory_space=pltpu.SMEM)
+    hbm = pl.BlockSpec(memory_space=pltpu.HBM)
     dma = pltpu.SemaphoreType.DMA
     return pl.pallas_call(
         kernel,
         out_shape=jax.ShapeDtypeStruct((3, TILES * TILE), F32),
-        in_specs=[vmem, vmem, vmem, smem, vmem, vmem, vmem, vmem, vmem, vmem, smem],
-        out_specs=vmem,
+        in_specs=[hbm] * 11,
+        out_specs=pl.BlockSpec(memory_space=pltpu.VMEM),
         scratch_shapes=[
+            pltpu.VMEM((3, TILES * TILE), F32),
+            pltpu.VMEM((3, 2, TILES * TILE), F32),
+            pltpu.VMEM((2, TILES), jnp.int32),
+            pltpu.SMEM((1, TILES), jnp.int32),
+            pltpu.VMEM((1, 256), jnp.int32),
+            pltpu.VMEM((TILES, TILE), jnp.int32),
+            pltpu.VMEM((128, 128), F32),
+            pltpu.VMEM((128, 384), F32),
+            pltpu.VMEM((1, 128), jnp.int32),
+            pltpu.VMEM((1, 128), jnp.int32),
+            pltpu.SMEM((1, 3), F32),
+            dma((11,)),
             pltpu.VMEM((2, TILES, 64, 256), BF16),
             pltpu.VMEM((3, TILES, TILE), F32),
             pltpu.VMEM((3, TILES, 128), F32),
@@ -490,16 +522,16 @@
             dma((2, 4)), dma((2, 4)), dma((2,)), dma((2,)),
         ],
         compiler_params=pltpu.CompilerParams(
-            collective_id=0, has_side_effects=True, vmem_limit_bytes=48 * 1024 * 1024
+            collective_id=0, has_side_effects=True, vmem_limit_bytes=60 * 1024 * 1024
         ),
         cost_estimate=pl.CostEstimate(
             flops=200_000_000, bytes_accessed=1_000_000, transcendentals=0
         ),
         name="substeps",
     )(
-        adjoint_end, positions, tile_brick, tile_fill.reshape(1, TILES), send_rows,
+        adjoint_end, jnp.swapaxes(positions, 0, 1), tile_brick, tile_fill.reshape(1, TILES), send_rows,
         source_rows.reshape(TILES, TILE), ckpt_mass, ckpt_velocity,
-        ckpt_target.reshape(1, 128), ckpt_brick.reshape(1, 128), gripper_axis,
+        ckpt_target.reshape(1, 128), ckpt_brick.reshape(1, 128), gripper_axis.reshape(1, 3),
     )
 
 

time: 47.9 us -> 44.6 us (0.931)
  Pallas kernels: 45.8 us -> 42.8 us
    pallas_call x1, Pallas kernels: 45.8 us -> 42.8 us  [per_device(): pl.pallas_call(kernel, out_shape=jax.ShapeDtypeStruct((3, TILES * TILE),...]
    unnamed x22 -> x1, local copies, waits for them, and re-layouts: 1.87 us -> 1.58 us
where the time goes in v1:
time: 44.6 us; the launch traced here: 44.4 us
  Pallas kernels  42.8 us (96%)
  local copies, waits for them, and re-layouts  1.58 us (4%)
    pallas_call x1, Pallas kernels, per_device(): pl.pallas_call(kernel, out_shape=jax.ShapeDtypeStruct((3, TILES * TILE),...  42.8 us
    unnamed x1, local copies, waits for them, and re-layouts  1.58 us

profile of v1, /device:TPU:24, one launch (start us, length us, event | category | flops | bytes accessed | tf_op | source)
XLA Modules:
  0.0 44.4 jit_solution(13825088326393737751)
XLA Ops:
  0.0 42.8 %substeps.1 = f32[3,8192]{1,0:T(4,128)} custom-call(f32[3,8192]{1,0:T(4,128)} %adj_hbm.1, f32[3,2,8192]{2,1,0:T(2,128)} %bitcast.6, s32[2,64]{1,0:T(2,128)} %tile_hbm.1, s32[1,64]{1,0:T(1,128)} %bitcast.8, s32[1,256]{1,0:T(1,128)} %send_hbm.1, s32[64,128]{1,0:T(8,128)} %bitcast.7, f32[128,128]{1,0:T(8,128)} %mass_hbm.1, f32[128,384]{1,0:T(8,128)} %vel_hbm.1, ...), custom_call_target="tpu_custom_call" | custom-call | flops 200000000 | bytes 1000000 | tf_op jit(solution)/shard_map/substeps/pallas_call | solution.py:482
  42.9 1.6 %copy.13 = f32[3,8192]{1,0:T(4,128)} copy(f32[3,8192]{1,0:T(4,128)} %substeps.1) | data formatting | bytes 196608

commit v2 on v1

--- a/solution.py
+++ b/solution.py
@@ -167,7 +167,6 @@
 
     pl.semaphore_wait(barrier, NXC - 1 + NZ - 1 + 4)
     run(NXC, lambda d: near_copy(s1a, r1a, a1s, a1r, d).start())
-    run(NXC, lambda d: near_copy(s1b, r1b, b1s, b1r, d).start())
     own = pl.ds(pl.multiple_of(xc * BLOCK, 8), BLOCK)
     r1a[own] = s1a[own]
     r1b[own] = s1b[own]
@@ -254,19 +253,36 @@
         y_low = remote(ys.at[k, 1], yr.at[k, 1], hs.at[k, 3], hr.at[k, 3], (b, down))
         return x_high, x_low, y_high, y_low
 
-    def send_halo(k):
-        xs[k, 0] = grid[pl.ds(3, 48, stride=4), :]
-        xs[k, 1] = grid[pl.ds(0, 48, stride=4), :]
-        cells = grid[...].reshape(12, 16, 128)
-        ys[k, 0] = cells[:, 12:16]
-        ys[k, 1] = cells[:, 0:4]
-        for copy in halo(k):
-            copy.start()
-
     brick_lane = iota((1, 128), 1)
     lane_x = lax.bitwise_and(brick_lane, 7)
     lane_y = lax.bitwise_and(lax.shift_right_logical(brick_lane, 3), 3)
     lane_z = lax.shift_right_logical(brick_lane, 5)
+    lane_y3 = lane_y.reshape(1, 1, 128)
+
+    def send_halo(k):
+        for side in range(2):
+            plane = grid[pl.ds(3 - 3 * side, 48, stride=4), :]
+            found = jnp.zeros((8, 128), F32)
+            for i in range(6):
+                part = plane[8 * i:8 * i + 8]
+                turn = (i - 7 + 7 * side) % 128
+                part = pltpu.roll(part, turn, 1) if turn else part
+                found = jnp.where(lane_x == i, part, found)
+            xs[k, side] = found
+        cells = grid[...].reshape(12, 16, 128)
+        for side in range(2):
+            plane = cells[:, 12 - 12 * side:16 - 12 * side]
+            found = plane[0:3]
+            found = pltpu.roll(found, 104, 2) if side == 0 else found
+            for i in range(1, 4):
+                part = plane[3 * i:3 * i + 3]
+                turn = (8 * i - 24 + 24 * side) % 128
+                part = pltpu.roll(part, turn, 2) if turn else part
+                found = jnp.where(lane_y3 == i, part, found)
+            ys[k, side] = found
+        for copy in halo(k):
+            copy.start()
+
     has_left = jnp.where(b > 0, 1.0, 0.0)
     has_right = jnp.where(b < N_BRICK - 1, 1.0, 0.0)
     has_down = jnp.where(s > 0, 1.0, 0.0)
@@ -274,19 +290,26 @@
 
     def smooth(k):
         planes = [grid[pl.ds(j, 48, stride=4), :] for j in range(4)]
-        before = jnp.where(
-            lane_x == 0, pltpu.roll(xr[k, 0] * has_left, 121, 1), pltpu.roll(planes[3], 1, 1)
-        )
-        after = jnp.where(
-            lane_x == 7, pltpu.roll(xr[k, 1] * has_right, 7, 1), pltpu.roll(planes[0], 127, 1)
-        )
+        came = xr[k, 0] * has_left
+        came = jnp.concatenate(
+            [came] + [pltpu.roll(came, 128 - i, 1) for i in range(1, 6)], axis=0
+        )
+        before = jnp.where(lane_x == 0, came, pltpu.roll(planes[3], 1, 1))
+        came = xr[k, 1] * has_right
+        came = jnp.concatenate([pltpu.roll(came, 7 - i, 1) for i in range(6)], axis=0)
+        after = jnp.where(lane_x == 7, came, pltpu.roll(planes[0], 127, 1))
         line = [before] + planes + [after]
         for j in range(4):
             xsum[pl.ds(j, 48, stride=4), :] = line[j] + line[j + 2]
         cells = grid[...].reshape(12, 16, 128)
-        low = pltpu.roll((yr[k, 0] * has_down), 104, 2)
-        high = pltpu.roll((yr[k, 1] * has_up), 24, 2)
-        lane_y3 = lane_y.reshape(1, 1, 128)
+        came = yr[k, 0] * has_down
+        low = jnp.concatenate(
+            [came] + [pltpu.roll(came, 128 - 8 * i, 2) for i in range(1, 4)], axis=0
+        )
+        came = yr[k, 1] * has_up
+        high = jnp.concatenate(
+            [pltpu.roll(came, 24 - 8 * i, 2) for i in range(3)] + [came], axis=0
+        )
         below = jnp.where(lane_y3 == 0, low, pltpu.roll(cells[:, 12:16], 8, 2))
         above = jnp.where(lane_y3 == 3, high, pltpu.roll(cells[:, 0:4], 120, 2))
         ysum = jnp.concatenate([cells[:, 4:16], above], axis=1) + jnp.concatenate(
@@ -306,10 +329,9 @@
             out.append(base + diffusion * (beside - 6.0 * base))
         return out
 
-    def relay(src, dst):
-        for i in range(NZ):
-            dst[i, 0:8, :] = src[pl.ds(i, 8, stride=BLOCK), :]
-            dst[i, 8:16, :] = src[pl.ds(16 + i, 8, stride=BLOCK), :]
+    def relay(src, dst, i):
+        dst[i, 0:8, :] = src[pl.ds(i, 8, stride=BLOCK), :]
+        dst[i, 8:16, :] = src[pl.ds(NZ + i, 8, stride=BLOCK), :]
 
     def by_node(got, place):
         value = got.reshape(256, 128)
@@ -359,7 +381,6 @@
     send_halo(1)
 
     run(NXC, lambda d: near_copy(s1a, r1a, a1s, a1r, d).wait_recv())
-    relay(r1a, s2a)
     index_in = r1a[pl.ds(32, 8, stride=BLOCK), :]
     index_two = jnp.concatenate([index_in, pltpu.roll(index_in, 112, 1)], axis=0)
     index_two = jnp.where(iota((16, 128), 1) < NZ, index_two, 0.0).astype(BF16)
@@ -369,13 +390,15 @@
     )
     for i in range(NZ):
         s2a[i, 16:17, :] = index_far[i:i + 1]
-    run(NZ, lambda d: far_copy(s2a, r2a, a2s, a2r, d).start())
+
+    def leave_a(d):
+        relay(r1a, s2a, far(d))
+        far_copy(s2a, r2a, a2s, a2r, d).start()
+
+    run(NZ, leave_a)
+    relay(r1a, s2a, z)
     r2a[z] = s2a[z]
-
-    run(NXC, lambda d: near_copy(s1b, r1b, b1s, b1r, d).wait_recv())
-    relay(r1b, s2b)
-    r2b[z] = s2b[z]
-    run(NZ, lambda d: far_copy(s2b, r2b, b2s, b2r, d).start())
+    run(NXC, lambda d: near_copy(s1b, r1b, b1s, b1r, d).start())
 
     def second_weights(g, carry):
         build(0, g)
@@ -424,6 +447,17 @@
     go_right = remote(ms.at[1], mr.at[0], gs.at[1], gr.at[1], (right, s))
     go_left.start()
     go_right.start()
+
+    run(NXC, lambda d: near_copy(s1b, r1b, b1s, b1r, d).wait_recv())
+
+    def leave_b(d):
+        relay(r1b, s2b, far(d))
+        far_copy(s2b, r2b, b2s, b2r, d).start()
+
+    run(NZ, leave_b)
+    relay(r1b, s2b, z)
+    r2b[z] = s2b[z]
+
     go_left.wait_recv()
     go_right.wait_recv()
     for v in range(8):
@@ -481,7 +515,7 @@
     dma = pltpu.SemaphoreType.DMA
     return pl.pallas_call(
         kernel,
-        out_shape=jax.ShapeDtypeStruct((3, TILES * TILE), F32),
+        out_shape=pltpu.VMEM((3, TILES * TILE), F32),
         in_specs=[hbm] * 11,
         out_specs=pl.BlockSpec(memory_space=pltpu.VMEM),
         scratch_shapes=[
@@ -511,10 +545,10 @@
             pltpu.VMEM((NZ, 17, 128), F32),
             pltpu.VMEM((NZ, 16, 128), F32),
             pltpu.VMEM((NZ, 16, 128), F32),
-            pltpu.VMEM((2, 2, 48, 128), F32),
-            pltpu.VMEM((2, 2, 48, 128), F32),
-            pltpu.VMEM((2, 2, 12, 4, 128), F32),
-            pltpu.VMEM((2, 2, 12, 4, 128), F32),
+            pltpu.VMEM((2, 2, 8, 128), F32),
+            pltpu.VMEM((2, 2, 8, 128), F32),
+            pltpu.VMEM((2, 2, 3, 4, 128), F32),
+            pltpu.VMEM((2, 2, 3, 4, 128), F32),
             pltpu.VMEM((2, 3, 128), F32),
             pltpu.VMEM((2, 3, 128), F32),
             dma((NXC,)), dma((NXC,)), dma((NXC,)), dma((NXC,)),

time: 44.6 us -> 41.3 us (0.926)
  Pallas kernels: 42.8 us -> 40.6 us
  local copies, waits for them, and re-layouts: 1.58 us -> 0.66 us
    pallas_call x1, Pallas kernels: 42.8 us -> 40.6 us  [per_device(): pl.pallas_call(kernel, out_shape=pltpu.VMEM((3, TILES * TILE), F32), in_s...]
    unnamed x1, local copies, waits for them, and re-layouts: 1.58 us -> 0.66 us
where the time goes in v2:
time: 41.3 us; the launch traced here: 41.2 us
  Pallas kernels  40.6 us (98%)
  local copies, waits for them, and re-layouts  0.66 us (2%)
    pallas_call x1, Pallas kernels, per_device(): pl.pallas_call(kernel, out_shape=pltpu.VMEM((3, TILES * TILE), F32), in_s...  40.6 us

profile of v2, /device:TPU:24, one launch (start us, length us, event | category | flops | bytes accessed | tf_op | source)
XLA Modules:
  0.0 41.2 jit_solution(9947075456447407852)
XLA Ops:
  0.0 40.6 %substeps.1 = f32[3,8192]{1,0:T(4,128)S(1)} custom-call(f32[3,8192]{1,0:T(4,128)} %adj_hbm.1, f32[3,2,8192]{2,1,0:T(2,128)} %bitcast.6, s32[2,64]{1,0:T(2,128)} %tile_hbm.1, s32[1,64]{1,0:T(1,128)} %bitcast.8, s32[1,256]{1,0:T(1,128)} %send_hbm.1, s32[64,128]{1,0:T(8,128)} %bitcast.7, f32[128,128]{1,0:T(8,128)} %mass_hbm.1, f32[128,384]{1,0:T(8,128)} %vel_hbm.1, ...), custom_call_target="tpu_custom_call" | custom-call | flops 200000000 | bytes 1000000 | tf_op jit(solution)/shard_map/substeps/pallas_call | solution.py:516
  40.6 0.7 %copy.13 = f32[3,8192]{1,0:T(4,128)} copy(f32[3,8192]{1,0:T(4,128)S(1)} %substeps.1) | data formatting | bytes 196608

commit v3 on v2

--- a/solution.py
+++ b/solution.py
@@ -12,7 +12,6 @@
 NXC = 8
 N_BRICK = 128
 N_SLAB = 4
-BLOCK = 40
 
 diffusion = 0.15
 F32 = jnp.float32
@@ -66,24 +65,24 @@
     up = lax.rem(s + 1, N_SLAB)
 
     def near(d):
-        return lax.rem(xc + d, NXC)
+        return lax.rem(xc + (4, 5, 3, 6, 2, 7, 1)[d - 1], NXC)
 
     def far(d):
-        turn = lax.div(d, 2) * (1 - 2 * lax.rem(d, 2))
-        return lax.rem(z + NZ + NZ // 2 + turn, NZ)
+        turn = (d // 2) * (1 - 2 * (d % 2))
+        return lax.rem(z + NZ + NZ // 2 + turn * (1 - 2 * lax.rem(xc, 2)), NZ)
 
     barrier = pltpu.get_barrier_semaphore()
 
-    def greet_near(d, carry):
+    def greet_near(d):
         pl.semaphore_signal(barrier, inc=1, device_id=(z * NXC + near(d), s), device_id_type=MESH)
-        return carry
-
-    def greet_far(d, carry):
+
+    def greet_far(d):
         pl.semaphore_signal(barrier, inc=1, device_id=(far(d) * NXC + xc, s), device_id_type=MESH)
-        return carry
-
-    lax.fori_loop(1, NZ, greet_far, 0)
-    lax.fori_loop(1, NXC, greet_near, 0)
+
+    for d in range(1, NZ):
+        greet_far(d)
+    for d in range(1, NXC):
+        greet_near(d)
     for who in ((left, s), (right, s), (b, down), (b, up)):
         pl.semaphore_signal(barrier, inc=1, device_id=who, device_id_type=MESH)
 
@@ -109,22 +108,15 @@
 
     def near_copy(src, dst, send, recv, d):
         to = near(d)
-        return remote(
-            src.at[pl.ds(pl.multiple_of(to * BLOCK, 8), BLOCK)],
-            dst.at[pl.ds(pl.multiple_of(xc * BLOCK, 8), BLOCK)],
-            send.at[d], recv.at[d], (z * NXC + to, s),
-        )
+        return remote(src.at[to], dst.at[xc], send.at[d], recv.at[d], (z * NXC + to, s))
 
     def far_copy(src, dst, send, recv, d):
         to = far(d)
         return remote(src.at[to], dst.at[z], send.at[d], recv.at[d], (to * NXC + xc, s))
 
     def run(count, act):
-        def body(d, carry):
+        for d in range(1, count):
             act(d)
-            return carry
-
-        lax.fori_loop(1, count, body, 0)
 
     lane = iota((8, 128), 1)
     axis = [jnp.full((1, 128), axis_ref[0, c], F32) for c in range(3)]
@@ -160,16 +152,14 @@
     index_right = jnp.where(iota((128, 128), 0) == within, 1.0, 0.0).astype(BF16)
     index_out = contract_last(index_left, index_right)
     for i in range(NXC):
-        s1a[BLOCK * i:BLOCK * i + 32, :] = packed[32 * i:32 * i + 32, 0:128]
-        s1a[BLOCK * i + 32:BLOCK * i + 40, :] = jnp.broadcast_to(index_out[i:i + 1], (8, 128))
-        s1b[BLOCK * i:BLOCK * i + 32, :] = packed[32 * i:32 * i + 32, 128:256]
-        s1b[BLOCK * i + 32:BLOCK * i + 40, :] = jnp.zeros((8, 128), F32)
+        s1a[i, 0:32, :] = packed[32 * i:32 * i + 32, 0:128]
+        s1a[i, 32:33, :] = index_out[i:i + 1]
+        s1b[i] = packed[32 * i:32 * i + 32, 128:256]
 
     pl.semaphore_wait(barrier, NXC - 1 + NZ - 1 + 4)
     run(NXC, lambda d: near_copy(s1a, r1a, a1s, a1r, d).start())
-    own = pl.ds(pl.multiple_of(xc * BLOCK, 8), BLOCK)
-    r1a[own] = s1a[own]
-    r1b[own] = s1b[own]
+    r1a[xc] = s1a[xc]
+    r1b[xc] = s1b[xc]
 
     for load in loads[5:11]:
         load.wait()
@@ -330,8 +320,10 @@
         return out
 
     def relay(src, dst, i):
-        dst[i, 0:8, :] = src[pl.ds(i, 8, stride=BLOCK), :]
-        dst[i, 8:16, :] = src[pl.ds(NZ + i, 8, stride=BLOCK), :]
+        for side in range(2):
+            dst[i, 8 * side:8 * side + 8, :] = jnp.concatenate(
+                [src[j, pl.ds(NZ * side + i, 1), :] for j in range(NXC)], axis=0
+            )
 
     def by_node(got, place):
         value = got.reshape(256, 128)
@@ -381,7 +373,7 @@
     send_halo(1)
 
     run(NXC, lambda d: near_copy(s1a, r1a, a1s, a1r, d).wait_recv())
-    index_in = r1a[pl.ds(32, 8, stride=BLOCK), :]
+    index_in = jnp.concatenate([r1a[j, 32:33, :] for j in range(NXC)], axis=0)
     index_two = jnp.concatenate([index_in, pltpu.roll(index_in, 112, 1)], axis=0)
     index_two = jnp.where(iota((16, 128), 1) < NZ, index_two, 0.0).astype(BF16)
     pick = jnp.where(iota((NZ, 128), 0) == iota((NZ, 128), 1), 1.0, 0.0).astype(BF16)
@@ -537,10 +529,10 @@
             pltpu.VMEM((192, 128), F32),
             pltpu.VMEM((192, 128), F32),
             pltpu.VMEM((6, TILES, 128), F32),
-            pltpu.VMEM((NXC * BLOCK, 128), F32),
-            pltpu.VMEM((NXC * BLOCK, 128), F32),
-            pltpu.VMEM((NXC * BLOCK, 128), F32),
-            pltpu.VMEM((NXC * BLOCK, 128), F32),
+            pltpu.VMEM((NXC, 33, 128), F32),
+            pltpu.VMEM((NXC, 33, 128), F32),
+            pltpu.VMEM((NXC, 32, 128), F32),
+            pltpu.VMEM((NXC, 32, 128), F32),
             pltpu.VMEM((NZ, 17, 128), F32),
             pltpu.VMEM((NZ, 17, 128), F32),
             pltpu.VMEM((NZ, 16, 128), F32),

time: 41.3 us -> 40.8 us (0.988); the launches traced: 41.2 us -> 40.3 us
  Pallas kernels: 40.6 us -> 39.6 us
    pallas_call x1, Pallas kernels: 40.6 us -> 39.6 us  [per_device(): pl.pallas_call(kernel, out_shape=pltpu.VMEM((3, TILES * TILE), F32), in_s...]
where the time goes in v3:
time: 40.8 us; the launch traced here: 40.3 us
  Pallas kernels  39.6 us (97%)
  local copies, waits for them, and re-layouts  0.66 us (2%)
    pallas_call x1, Pallas kernels, per_device(): pl.pallas_call(kernel, out_shape=pltpu.VMEM((3, TILES * TILE), F32), in_s...  39.6 us

profile of v3, /device:TPU:24, one launch (start us, length us, event | category | flops | bytes accessed | tf_op | source)
XLA Modules:
  0.0 40.3 jit_solution(15409637792847415816)
XLA Ops:
  0.0 39.6 %substeps.1 = f32[3,8192]{1,0:T(4,128)S(1)} custom-call(f32[3,8192]{1,0:T(4,128)} %adj_hbm.1, f32[3,2,8192]{2,1,0:T(2,128)} %bitcast.6, s32[2,64]{1,0:T(2,128)} %tile_hbm.1, s32[1,64]{1,0:T(1,128)} %bitcast.8, s32[1,256]{1,0:T(1,128)} %send_hbm.1, s32[64,128]{1,0:T(8,128)} %bitcast.7, f32[128,128]{1,0:T(8,128)} %mass_hbm.1, f32[128,384]{1,0:T(8,128)} %vel_hbm.1, ...), custom_call_target="tpu_custom_call" | custom-call | flops 200000000 | bytes 1000000 | tf_op jit(solution)/shard_map/substeps/pallas_call | solution.py:508
  39.6 0.7 %copy.13 = f32[3,8192]{1,0:T(4,128)} copy(f32[3,8192]{1,0:T(4,128)S(1)} %substeps.1) | data formatting | bytes 196608
